TPU v7x, 32 devices: a whole 2x2x4 slice. The times are simulated.
32 devices in a mesh: grp: 2 (over x), lon: 16 (over z, y, core).
Axes of the slice: x: 2, y: 2, z: 4, core: 2. Of those that a mesh axis runs over, the one named last changes fastest.
Arguments:
- latent: bfloat16 [128, 256, 1024], P('grp', 'lon'), parts along dimension 0, may hold values from -6 to 6
- filters: bfloat16 [9, 128, 256], replicated, may hold values from -0.375 to 0.375
- quadrature: float32 [64], replicated, may hold values from 0.3 to 3
- basis_values: bfloat16 [128, 8, 64, 32], replicated, may hold values from -0.375 to 0.375
- source_row: int32 [128, 8], replicated, may hold values from 0 to 63, as said below
- offset: int32 [128, 8], replicated, may hold values from -1 to 1
- basis_index: int32 [128, 8], replicated, may hold values from 0 to 8
- across_pole: int32 [128, 8], replicated, may hold values from 0 to 1, as said below
Outputs:
- upsampled: bfloat16 [256, 2048, 128], P('grp', 'lon'), parts along dimension 0
There are 2 independent parts, one for each index of `grp`. A program takes and returns all parts, laid end to end along the dimension named above; an argument that names none is the same for every part. Nothing has to cross between parts.
Inputs may be any that keep to these rules, and one draw needn't show every extreme that they name: Where across_pole is 1, source_row is under 16; elsewhere it lies within one of h / 2 for output row h (clipped to the rows). across_pole is 1 only in the first 32 output rows.
All inputs are finite; a program needn't handle non-finite values.
Results may differ from a plain program's by a relative error of at most 0.0065.
Values may be sent and summed in bfloat16 or wider, within the bound.
A program may use at most 256 MiB of HBM per device.

v0:
```python
import functools

import jax
import jax.numpy as jnp
from jax import lax
from jax.experimental import pallas as pl
from jax.experimental.pallas import tpu as pltpu
from jax.sharding import PartitionSpec as P

BLOCK = 32
FINE = 64
MIX_ROWS = 4
OUT_ROWS = 8


def from_behind(block, axis, distance):
    devices = range(lax.axis_size(axis))
    route = [((i - distance) % len(devices), i) for i in devices]
    return lax.ppermute(block, axis, route)


def compute(mix_steps, bases, entries, rows_ref, starts_ref, quad_ref, ext_ref, filt_ref, values_ref, out_ref, mixed):
    step = pl.program_id(0)
    channels = out_ref.shape[2]

    @pl.when(step < mix_steps)
    def _():
        for r in range(MIX_ROWS):
            row = step * MIX_ROWS + r
            product = lax.dot_general(
                ext_ref[r], filt_ref[...], (((0,), (0,)), ((), ())), preferred_element_type=jnp.float32
            )
            product = (product * quad_ref[row]).astype(jnp.bfloat16)
            for k in range(bases):
                mixed[row * bases + k] = product[:, k * channels : (k + 1) * channels]

    @pl.when(step >= mix_steps)
    def _():
        for g in range(OUT_ROWS):
            h = (step - mix_steps) * OUT_ROWS + g
            parts = []
            for j in range(entries):
                e = h * entries + j
                start = pl.multiple_of(starts_ref[e], BLOCK)
                parts.append(mixed[rows_ref[e], pl.ds(start, 2 * BLOCK), :])
            first = jnp.concatenate([p[:BLOCK] for p in parts], axis=0)
            second = jnp.concatenate([p[BLOCK:] for p in parts], axis=0)
            terms = jnp.concatenate([first, second], axis=1)
            values = jnp.concatenate([values_ref[g, j] for j in range(entries)], axis=1)
            total = jnp.dot(values, terms, preferred_element_type=jnp.float32)
            total = total.astype(jnp.bfloat16)
            out_ref[g, :FINE] = total[:, :channels]
            out_ref[g, FINE:] = total[:, channels:]


def on_device(
    latent, filters, quadrature, basis_values, source_row, offset, basis_index, across_pole
):
    source_total = latent.shape[0]
    row_total, entries = source_row.shape
    bases, channels, deep = filters.shape
    pole_source = source_total // 4
    half = latent.shape[2] // 2
    turned = jnp.roll(latent[:pole_source], half, axis=2)
    stacked = jnp.concatenate([latent, turned], axis=0)
    tile = lax.all_to_all(stacked, "lon", split_axis=2, concat_axis=1, tiled=True)
    left = from_behind(tile[:, :, BLOCK:], "lon", 1)
    right = from_behind(tile[:, :, :BLOCK], "lon", -1)
    ext = jnp.concatenate([left, tile, right], axis=2)
    rows = ((source_row + source_total * across_pole) * bases + basis_index).reshape(-1)
    starts = ((1 - offset) * BLOCK).reshape(-1)
    quad = jnp.concatenate([quadrature, quadrature[:pole_source]])
    filt = filters.reshape(bases * channels, deep).T
    all_rows = source_total + pole_source
    mix_steps = all_rows // MIX_ROWS
    out_steps = row_total // OUT_ROWS
    smem = pl.BlockSpec(memory_space=pltpu.SMEM)
    width = ext.shape[2]
    last = lambda i: jnp.maximum(i - mix_steps, 0)
    return pl.pallas_call(
        functools.partial(compute, mix_steps, bases, entries),
        grid=(mix_steps + out_steps,),
        out_shape=jax.ShapeDtypeStruct((row_total, 2 * FINE, channels), jnp.bfloat16),
        in_specs=[
            smem,
            smem,
            smem,
            pl.BlockSpec((MIX_ROWS, deep, width), lambda i: (jnp.minimum(i, mix_steps - 1), 0, 0)),
            pl.BlockSpec((deep, bases * channels), lambda i: (0, 0)),
            pl.BlockSpec((OUT_ROWS, entries, FINE, BLOCK), lambda i: (last(i), 0, 0, 0)),
        ],
        out_specs=pl.BlockSpec((OUT_ROWS, 2 * FINE, channels), lambda i: (last(i), 0, 0)),
        scratch_shapes=[pltpu.VMEM((all_rows * bases, width, channels), jnp.bfloat16)],
        compiler_params=pltpu.CompilerParams(vmem_limit_bytes=48 * 2**20),
    )(rows, starts, quad, ext, filt, basis_values)


def solution(mesh):
    in_specs = (P("grp", "lon", None), P(), P(), P(), P(), P(), P(), P())
    out_specs = P("grp", "lon", None)
    return jax.shard_map(
        on_device, mesh=mesh, in_specs=in_specs, out_specs=out_specs, check_vma=False
    )
```

profile of v0, /device:TPU:0, one launch (start us, length us, event | category | flops | bytes accessed | tf_op | source)
XLA Modules:
  0.0 214.8 jit_solution(14917351120593722869)
XLA Ops:
  0.0 1.1 fusion.1
  1.1 1.9 maximum_maximum_fusion
  2.9 5.1 %copy.32 = bf16[80,16,1024]{0,1,2:T(8,128)(2,1)} copy(bf16[80,16,1024]{2,1,0:T(8,128)(2,1)S(1)} %maximum_maximum_fusion) | data formatting | bytes 5242880 | tf_op jit(solution)/shard_map/concatenate | solution.py:65
  8.0 99.7 %all_to_all.18 = bf16[80,16,1024]{0,1,2:T(8,128)(2,1)} all-to-all(bf16[80,16,1024]{0,1,2:T(8,128)(2,1)} %copy.32), channel_id=1, replica_groups=mesh['grp'=2,'lon'=16] {'lon'}, dimensions={2} | all-to-all | bytes 5242880 | tf_op jit(solution)/shard_map/all_to_all | solution.py:66
  107.8 11.6 %copy.34 = bf16[80,16,16,64]{3,2,1,0:T(8,128)(2,1)} copy(bf16[80,16,16,64]{0,2,3,1:T(8,128)(2,1)} %bitcast.11) | data formatting | bytes 5242880 | tf_op jit(solution)/shard_map/all_to_all | solution.py:66
  119.3 9.8 %fusion = (bf16[80,256,32]{2,1,0:T(8,128)(2,1)}, bf16[80,256,32]{2,1,0:T(8,128)(2,1)}) fusion(bf16[80,256,64]{2,1,0:T(8,128)(2,1)} %bitcast.9), kind=kLoop, calls=%fused_computation.5 | loop fusion | bytes 5242880 | tf_op jit(solution)/shard_map/slice | solution.py:67
  129.1 0.0 copy-start
  129.1 0.0 copy-start.1
  129.1 0.0 copy-start.2
  129.1 4.7 %copy.35 = bf16[80,256,32]{1,2,0:T(8,128)(2,1)S(1)} copy(bf16[80,256,32]{2,1,0:T(8,128)(2,1)} %get-tuple-element.5) | data formatting | bytes 2621440 | tf_op jit(solution)/shard_map/slice | solution.py:67
  133.8 0.8 collective-permute-start
  134.6 5.7 %copy.36 = bf16[80,256,32]{1,2,0:T(8,128)(2,1)} copy(bf16[80,256,32]{2,1,0:T(8,128)(2,1)} %get-tuple-element.6) | data formatting | bytes 2621440 | tf_op jit(solution)/shard_map/slice | solution.py:68
  140.3 3.7 %collective-permute-start.1 = (bf16[80,256,32]{1,2,0:T(8,128)(2,1)}, bf16[80,256,32]{1,2,0:T(8,128)(2,1)}, u32[]{:S(2)}, u32[]{:S(2)}) collective-permute-start(bf16[80,256,32]{1,2,0:T(8,128)(2,1)} %copy.36), channel_id=1, source_target_pairs={{1,0},{2,1},{3,2},{4,3},{5,4},{6,5},{7,6},{8,7},{9,8},{10,9},{11,1... | collective-permute-start | bytes 3932168 | tf_op jit(solution)/shard_map/ppermute | solution.py:19
  144.0 0.0 copy-done
  144.0 0.1 copy.31
  144.1 0.1 reshape.10.starts_ref
  144.2 0.0 copy-done.1
  144.2 0.0 copy-done.2
  144.2 0.0 copy-done.3
  144.2 0.1 copy.30
  144.3 0.1 reshape.9.rows_ref
  144.4 1.4 copy.39
  145.8 0.0 copy-start.4
  145.8 23.1 %copy.40.values_ref = bf16[128,8,64,32]{3,2,1,0:T(8,128)(2,1)} copy(bf16[128,8,64,32]{0,3,2,1:T(8,128)(2,1)} %param.11) | data formatting | bytes 8388608 | tf_op args[3]
  168.9 0.0 copy-done.4
  168.9 0.1 pad_maximum_fusion.1.quad_ref
  169.0 0.0 collective-permute-done
  169.0 4.1 %copy.37 = bf16[80,256,32]{2,1,0:T(8,128)(2,1)} copy(bf16[80,256,32]{1,2,0:T(8,128)(2,1)S(1)} %collective-permute-done) | data formatting | bytes 2621440 | tf_op jit(solution)/shard_map/ppermute | solution.py:19
  173.1 0.0 collective-permute-done.1
  173.1 5.2 %copy.38 = bf16[80,256,32]{2,1,0:T(8,128)(2,1)} copy(bf16[80,256,32]{1,2,0:T(8,128)(2,1)} %collective-permute-done.1) | data formatting | bytes 2621440 | tf_op jit(solution)/shard_map/ppermute | solution.py:19
  178.3 8.3 %pad_maximum_fusion.ext_ref = bf16[80,256,128]{2,1,0:T(8,128)(2,1)S(1)} fusion(bf16[80,256,32]{2,1,0:T(8,128)(2,1)} %copy.38, bf16[80,256,64]{2,1,0:T(8,128)(2,1)} %bitcast.10, bf16[80,256,32]{2,1,0:T(8,128)(2,1)} %copy.37), kind=kLoop, calls=%fused_computation | loop fusion | flops 15728640 | bytes 10485760 | tf_op jit(solution)/shard_map/concatenate | solution.py:69
  186.6 28.2 %shard_map.82 = bf16[128,128,128]{2,1,0:T(8,128)(2,1)} custom-call(s32[1024]{0:T(1024)S(1)} %reshape.9.rows_ref, s32[1024]{0:T(1024)S(1)} %reshape.10.starts_ref, f32[80]{0:T(128)S(1)} %pad_maximum_fusion.1.quad_ref, bf16[80,256,128]{2,1,0:T(8,128)(2,1)S(1)} %pad_maximum_fusion.ext_ref, bf16[256,1152]{1,0:T(8,128)(2,1)S(1)} %bitcast.8, ...), custom_call_target="tpu_custom_call" | custom-call | tf_op jit(solution)/shard_map/pallas_call | solution.py:80
  (3 shorter events, 0.0 us)
Async XLA Ops:
  129.1 14.9 %copy-start = (s32[128,8]{0,1:T(8,128)S(1)}, s32[128,8]{0,1:T(8,128)}, u32[]{:S(2)}) copy-start(s32[128,8]{0,1:T(8,128)} %param.13) | copy-start | bytes 12292
  129.1 15.1 %copy-start.1 = (s32[128,8]{0,1:T(8,128)S(1)}, s32[128,8]{0,1:T(8,128)}, u32[]{:S(2)}) copy-start(s32[128,8]{0,1:T(8,128)} %param.14) | copy-start | bytes 12292
  129.1 15.1 %copy-start.2 = (s32[128,8]{0,1:T(8,128)S(1)}, s32[128,8]{0,1:T(8,128)}, u32[]{:S(2)}) copy-start(s32[128,8]{0,1:T(8,128)} %param.12) | copy-start | bytes 12292
  129.1 15.1 %copy-start.3 = (s32[128,8]{0,1:T(8,128)S(1)}, s32[128,8]{0,1:T(8,128)}, u32[]{:S(2)}) copy-start(s32[128,8]{0,1:T(8,128)} %param.15) | copy-start | bytes 12292
  133.8 35.2 %collective-permute-start = (bf16[80,256,32]{1,2,0:T(8,128)(2,1)S(1)}, bf16[80,256,32]{1,2,0:T(8,128)(2,1)S(1)}, u32[]{:S(2)}, u32[]{:S(2)}) collective-permute-start(bf16[80,256,32]{1,2,0:T(8,128)(2,1)S(1)} %copy.35), channel_id=1, source_target_pairs={{15,0},{0,1},{1,2},{2,3},{3,4},{4,5},{5,6},{6,7},{7,8},{8,9},{9,10... | collective-permute-start | bytes 3932168 | tf_op jit(solution)/shard_map/ppermute | solution.py:19
  140.3 32.8 %collective-permute-start.1 = (bf16[80,256,32]{1,2,0:T(8,128)(2,1)}, bf16[80,256,32]{1,2,0:T(8,128)(2,1)}, u32[]{:S(2)}, u32[]{:S(2)}) collective-permute-start(bf16[80,256,32]{1,2,0:T(8,128)(2,1)} %copy.36), channel_id=1, source_target_pairs={{1,0},{2,1},{3,2},{4,3},{5,4},{6,5},{7,6},{8,7},{9,8},{10,9},{11,1... | collective-permute-start | bytes 3932168 | tf_op jit(solution)/shard_map/ppermute | solution.py:19
  145.8 23.1 %copy-start.4 = (f32[64]{0:T(128)S(1)}, f32[64]{0:T(128)}, u32[]{:S(2)}) copy-start(f32[64]{0:T(128)} %param.10) | copy-start | bytes 772
where the time goes:
time: 216 us; the launch traced here: 215 us
  blocking collectives  99.7 us (46%)
  local copies, waits for them, and re-layouts  72 us (33%)
  Pallas kernels  28.2 us (13%)
  other arithmetic  10.2 us (5%)
  starting transfers between devices  4.49 us (2%)
    all_to_all x1, blocking collectives, on_device(): lax.all_to_all(stacked, 'lon', split_axis=2, concat_axis=1, tiled=True)  99.7 us
    pallas_call x1, Pallas kernels, on_device(): pl.pallas_call(functools.partial(compute, mix_steps, bases, entries), gri...  28.2 us
    unnamed x11, local copies, waits for them, and re-layouts  23.1 us
    slice x2, local copies, waits for them, and re-layouts, on_device(): left = from_behind(tile[:, :, BLOCK:], 'lon', 1)  14.5 us
    all_to_all x1, local copies, waits for them, and re-layouts, on_device(): lax.all_to_all(stacked, 'lon', split_axis=2, concat_axis=1, tiled=True)  11.6 us
    ppermute x2, local copies, waits for them, and re-layouts, from_behind(): return lax.ppermute(block, axis, route)  9.3 us
    concatenate x1, other arithmetic, on_device(): ext = jnp.concatenate([left, tile, right], axis=2)  8.29 us
    slice x1, local copies, waits for them, and re-layouts, on_device(): right = from_behind(tile[:, :, :BLOCK], 'lon', -1)  5.68 us
  transfers between devices with their start and end apart: 2, of which 0 were waited for; matrix products, arithmetic and copies ran while one was open for 16% of the time, Pallas kernels for 0%

commit v1 on v0

--- a/solution.py
+++ b/solution.py
@@ -11,6 +11,7 @@
 FINE = 64
 MIX_ROWS = 4
 OUT_ROWS = 8
+MESH = pl.DeviceIdType.MESH
 
 
 def from_behind(block, axis, distance):
@@ -95,9 +96,228 @@
     )(rows, starts, quad, ext, filt, basis_values)
 
 
+def exchange(axis, lat_ref, recv, from_left, from_right, pack, go_right, go_left, sends, recvs, halo_sends, halo_recvs):
+    n = lax.axis_size(axis)
+    me = lax.axis_index(axis)
+    right, left = lax.rem(me + 1, n), lax.rem(me + n - 1, n)
+    pairs = lat_ref.shape[0] // 8
+    sections = lat_ref.shape[0] // (2 * pairs) + 1
+    quads = pairs // 2
+    deep = go_right.shape[1]
+    channels = lat_ref.shape[1]
+
+    barrier = pltpu.get_barrier_semaphore()
+
+    @pl.loop(1, n)
+    def _(distance):
+        peer = lax.rem(me + distance, n)
+        pl.semaphore_signal(barrier, inc=1, device_id={axis: peer}, device_id_type=MESH)
+
+    pl.semaphore_wait(barrier, n - 1)
+
+    def source(section, target):
+        if section == 1:
+            return pack.at[lax.rem(target + n // 2, n), pl.ds(0, pairs)]
+        return pack.at[target, pl.ds(max(section - 1, 0) * pairs, pairs)]
+
+    def piece(section, target, sender, peer):
+        return pltpu.make_async_remote_copy(
+            src_ref=source(section, target),
+            dst_ref=recv.at[pl.ds(section * pairs, pairs), sender],
+            send_sem=sends.at[section, target],
+            recv_sem=recvs.at[section, sender],
+            device_id={axis: peer},
+            device_id_type=MESH,
+        )
+
+    def halo(section, way):
+        held, landed, peer = (go_right, from_left, right) if way == 0 else (go_left, from_right, left)
+        part = pl.ds(section * quads, quads)
+        return pltpu.make_async_remote_copy(
+            src_ref=held.at[part],
+            dst_ref=landed.at[part],
+            send_sem=halo_sends.at[section, way],
+            recv_sem=halo_recvs.at[section, way],
+            device_id={axis: peer},
+            device_id_type=MESH,
+        )
+
+    for section in range(sections):
+        if section != 1:
+            first = max(section - 1, 0) * pairs
+
+            @pl.loop(first, first + pairs)
+            def _(p):
+                for t in range(n // 2):
+                    a = lat_ref[2 * p, :, t * 128 : (t + 1) * 128]
+                    b = lat_ref[2 * p + 1, :, t * 128 : (t + 1) * 128]
+                    pack[2 * t, p] = jnp.concatenate([a[:, :64], b[:, :64]], axis=1)
+                    pack[2 * t + 1, p] = jnp.concatenate([a[:, 64:], b[:, 64:]], axis=1)
+
+        @pl.loop(1, n)
+        def _(distance):
+            peer = lax.rem(me + distance, n)
+            piece(section, peer, me, peer).start()
+
+        recv[pl.ds(section * pairs, pairs), me] = source(section, me)[...]
+
+    for section in range(sections):
+
+        @pl.loop(1, n)
+        def _(distance):
+            peer = lax.rem(me + n - distance, n)
+            piece(section, peer, peer, peer).wait_recv()
+
+        @pl.loop(section * quads, (section + 1) * quads)
+        def _(q):
+            pa = recv[2 * q].reshape(deep, 128)
+            pb = recv[2 * q + 1].reshape(deep, 128)
+            go_right[q] = jnp.concatenate([pa[:, 32:64], pa[:, 96:], pb[:, 32:64], pb[:, 96:]], axis=1)
+            go_left[q] = jnp.concatenate([pa[:, :32], pa[:, 64:96], pb[:, :32], pb[:, 64:96]], axis=1)
+
+        halo(section, 0).start()
+        halo(section, 1).start()
+
+    for section in range(sections):
+        halo(section, 0).wait_recv()
+        halo(section, 1).wait_recv()
+    for section in range(sections):
+        halo(section, 0).wait_send()
+        halo(section, 1).wait_send()
+
+        @pl.loop(1, n)
+        def _(distance):
+            peer = lax.rem(me + distance, n)
+            piece(section, peer, me, peer).wait_send()
+
+
+def exchanged(latent, axis):
+    n = lax.axis_size(axis)
+    rows, channels, _ = latent.shape
+    pairs = rows // 2 + rows // 8
+    quads = pairs // 2
+    sections = 5
+    deep = n * channels
+    kind = latent.dtype
+    vmem = pl.BlockSpec(memory_space=pltpu.VMEM)
+    recv, from_left, from_right = pl.pallas_call(
+        functools.partial(exchange, axis),
+        out_shape=[
+            jax.ShapeDtypeStruct((pairs, n, channels, 128), kind),
+            jax.ShapeDtypeStruct((quads, deep, 128), kind),
+            jax.ShapeDtypeStruct((quads, deep, 128), kind),
+        ],
+        in_specs=[vmem],
+        out_specs=[vmem] * 3,
+        scratch_shapes=[
+            pltpu.VMEM((n, rows // 2, channels, 128), kind),
+            pltpu.VMEM((quads, deep, 128), kind),
+            pltpu.VMEM((quads, deep, 128), kind),
+            pltpu.SemaphoreType.DMA((sections, n)),
+            pltpu.SemaphoreType.DMA((sections, n)),
+            pltpu.SemaphoreType.DMA((sections, 2)),
+            pltpu.SemaphoreType.DMA((sections, 2)),
+        ],
+        compiler_params=pltpu.CompilerParams(
+            collective_id=0, has_side_effects=True, vmem_limit_bytes=32 * 2**20
+        ),
+    )(latent)
+    return recv.reshape(pairs, deep, 128), from_left, from_right
+
+
+def spread(step, bases, entries, rows_ref, starts_ref, values_ref, out_ref, mixed):
+    channels = out_ref.shape[2]
+    for g in range(OUT_ROWS):
+        h = step * OUT_ROWS + g
+        parts = []
+        for j in range(entries):
+            e = h * entries + j
+            start = pl.multiple_of(starts_ref[e], BLOCK)
+            parts.append(mixed[rows_ref[e], pl.ds(start, 2 * BLOCK), :])
+        first = jnp.concatenate([p[:BLOCK] for p in parts], axis=0)
+        second = jnp.concatenate([p[BLOCK:] for p in parts], axis=0)
+        terms = jnp.concatenate([first, second], axis=1)
+        total = lax.dot_general(
+            values_ref[g], terms, (((0,), (0,)), ((), ())), preferred_element_type=jnp.float32
+        ).astype(jnp.bfloat16)
+        out_ref[g, :FINE] = total[:, :channels]
+        out_ref[g, FINE:] = total[:, channels:]
+
+
+def compute_packed(mix_steps, bases, entries, rows_ref, starts_ref, quad_ref, own_ref, left_ref, right_ref, filt_ref, values_ref, out_ref, mixed):
+    step = pl.program_id(0)
+    channels = out_ref.shape[2]
+
+    def mix(data, first_row, count, to):
+        size = 128 // count
+        product = lax.dot_general(
+            data, filt_ref[...], (((0,), (0,)), ((), ())), preferred_element_type=jnp.float32
+        )
+        for r in range(count):
+            row = first_row + r
+            part = (product[r * size : (r + 1) * size] * quad_ref[row]).astype(jnp.bfloat16)
+            for k in range(bases):
+                mixed[row * bases + k, to : to + size] = part[:, k * channels : (k + 1) * channels]
+
+    @pl.when(step < mix_steps)
+    def _():
+        mix(left_ref[0], step * 4, 4, 0)
+        mix(own_ref[0], step * 4, 2, BLOCK)
+        mix(own_ref[1], step * 4 + 2, 2, BLOCK)
+        mix(right_ref[0], step * 4, 4, 3 * BLOCK)
+
+    @pl.when(step >= mix_steps)
+    def _():
+        spread(step - mix_steps, bases, entries, rows_ref, starts_ref, values_ref, out_ref, mixed)
+
+
+def on_device_packed(
+    latent, filters, quadrature, basis_values, source_row, offset, basis_index, across_pole
+):
+    source_total = latent.shape[0]
+    row_total, entries = source_row.shape
+    bases, channels, deep = filters.shape
+    pole = source_total // 4
+    own, from_left, from_right = exchanged(latent, "lon")
+    place = jnp.where((source_row >= pole) | (across_pole == 1), source_row + pole, source_row)
+    rows = (place * bases + basis_index).reshape(-1)
+    starts = ((1 - offset) * BLOCK).reshape(-1)
+    quad = jnp.concatenate([quadrature[:pole], quadrature])
+    filt = filters.reshape(bases * channels, deep).T
+    values = jnp.swapaxes(basis_values, 2, 3).reshape(row_total, entries * BLOCK, FINE)
+    all_rows = source_total + pole
+    mix_steps = all_rows // 4
+    out_steps = row_total // OUT_ROWS
+    smem = pl.BlockSpec(memory_space=pltpu.SMEM)
+    last = lambda i: jnp.maximum(i - mix_steps, 0)
+    mixing = lambda i: (jnp.minimum(i, mix_steps - 1), 0, 0)
+    return pl.pallas_call(
+        functools.partial(compute_packed, mix_steps, bases, entries),
+        grid=(mix_steps + out_steps,),
+        out_shape=jax.ShapeDtypeStruct((row_total, 2 * FINE, channels), jnp.bfloat16),
+        in_specs=[
+            smem,
+            smem,
+            smem,
+            pl.BlockSpec((2, deep, 128), mixing),
+            pl.BlockSpec((1, deep, 128), mixing),
+            pl.BlockSpec((1, deep, 128), mixing),
+            pl.BlockSpec((deep, bases * channels), lambda i: (0, 0)),
+            pl.BlockSpec((OUT_ROWS, entries * BLOCK, FINE), lambda i: (last(i), 0, 0)),
+        ],
+        out_specs=pl.BlockSpec((OUT_ROWS, 2 * FINE, channels), lambda i: (last(i), 0, 0)),
+        scratch_shapes=[pltpu.VMEM((all_rows * bases, 4 * BLOCK, channels), jnp.bfloat16)],
+        compiler_params=pltpu.CompilerParams(vmem_limit_bytes=48 * 2**20),
+    )(rows, starts, quad, own, from_left, from_right, filt, values)
+
+
 def solution(mesh):
+    def chosen(latent, *rest):
+        packed = latent.shape[1] % 16 == 0
+        return (on_device_packed if packed else on_device)(latent, *rest)
+
     in_specs = (P("grp", "lon", None), P(), P(), P(), P(), P(), P(), P())
     out_specs = P("grp", "lon", None)
     return jax.shard_map(
-        on_device, mesh=mesh, in_specs=in_specs, out_specs=out_specs, check_vma=False
+        chosen, mesh=mesh, in_specs=in_specs, out_specs=out_specs, check_vma=False
     )

time: 216 us -> 141 us (0.65)
  blocking collectives: 99.7 us -> 0 us
  Pallas kernels: 28.2 us -> 114 us
  local copies, waits for them, and re-layouts: 72 us -> 23.8 us
  other arithmetic: 10.2 us -> 2.22 us
  starting transfers between devices: 4.49 us -> 0 us
    all_to_all x1 -> x0, blocking collectives: 99.7 us -> none  [on_device(): lax.all_to_all(stacked, 'lon', split_axis=2, concat_axis=1, tiled=True)]
    pallas_call x1 -> x2, Pallas kernels: 28.2 us -> 114 us  [the longest x1 88.2 us: exchanged(): pl.pallas_call(functools.partial(exchange, axis), out_shape=[jax.ShapeDty...]
    slice x4 -> x0, local copies, waits for them, and re-layouts: 21.2 us -> none  [the longest x2 14.5 us: on_device(): left = from_behind(tile[:, :, BLOCK:], 'lon', 1)]
    unnamed x11 -> x10, local copies, waits for them, and re-layouts: 23.1 us -> 6.42 us
    transpose x0 -> x1, local copies, waits for them, and re-layouts: none -> 15.6 us  [on_device_packed(): jnp.swapaxes(basis_values, 2, 3).reshape(row_total, entries * BLOCK, FINE)]
    all_to_all x1 -> x0, local copies, waits for them, and re-layouts: 11.6 us -> none  [on_device(): lax.all_to_all(stacked, 'lon', split_axis=2, concat_axis=1, tiled=True)]
    concatenate x3 -> x1, other arithmetic: 10.2 us -> 0.8 us  [on_device_packed(): quad = jnp.concatenate([quadrature[:pole], quadrature])]
    ppermute x2 -> x0, local copies, waits for them, and re-layouts: 9.3 us -> none  [from_behind(): return lax.ppermute(block, axis, route)]
  transfers between devices with their start and end apart: 2 -> 0, of which waited for: 0 -> 0; matrix products, arithmetic and copies ran while one was open for 16% -> 0% of each run, Pallas kernels for 0% -> 0%
where the time goes in v1:
time: 141 us; the launch traced here: 140 us
  Pallas kernels  114 us (81%)
  local copies, waits for them, and re-layouts  23.8 us (17%)
  other arithmetic  2.22 us (2%)
    pallas_call x1, Pallas kernels, exchanged(): pl.pallas_call(functools.partial(exchange, axis), out_shape=[jax.ShapeDty...  88.2 us
    pallas_call x1, Pallas kernels, on_device_packed(): pl.pallas_call(functools.partial(compute_packed, mix_steps, bases, entrie...  25.8 us
    transpose x1, local copies, waits for them, and re-layouts, on_device_packed(): jnp.swapaxes(basis_values, 2, 3).reshape(row_total, entries * BLOCK, FINE)  15.6 us
    unnamed x10, local copies, waits for them, and re-layouts  6.42 us

profile of v1, /device:TPU:0, one launch (start us, length us, event | category | flops | bytes accessed | tf_op | source)
XLA Modules:
  0.0 140.0 jit_solution(13537208166778596369)
XLA Ops:
  0.0 0.8 pad_maximum_fusion.quad_ref
  0.8 0.7 fusion.1
  1.5 0.7 subtract_multiply_fusion
  2.2 0.1 copy.12
  2.3 0.1 reshape.16.starts_ref
  2.4 0.1 copy.11
  2.5 0.1 reshape.15.rows_ref
  2.6 1.4 copy.13
  4.0 0.0 copy-start
  4.0 1.6 %copy-done = bf16[64,16,1024]{2,1,0:T(8,128)(2,1)S(1)} copy-done((bf16[64,16,1024]{2,1,0:T(8,128)(2,1)S(1)}, bf16[64,16,1024]{2,1,0:T(8,128)(2,1)}, u32[]{:S(2)}) %copy-start) | copy-done | bytes 2097176
  5.6 88.2 %shard_map.82 = (bf16[40,16,16,128]{3,2,1,0:T(8,128)(2,1)S(1)}, bf16[20,256,128]{2,1,0:T(8,128)(2,1)S(1)}, bf16[20,256,128]{2,1,0:T(8,128)(2,1)S(1)}) custom-call(bf16[64,16,1024]{2,1,0:T(8,128)(2,1)S(1)} %copy-done), custom_call_target="tpu_custom_call" | custom-call | tf_op jit(solution)/shard_map/pallas_call | solution.py:203
  93.7 0.0 copy-start.1
  93.7 1.0 copy-done.1
  94.8 0.0 copy-start.3
  94.8 1.1 copy-done.3
  95.9 15.6 %copy.14 = bf16[128,8,32,64]{3,2,1,0:T(8,128)(2,1)} copy(bf16[128,8,32,64]{0,2,3,1:T(8,128)(2,1)} %bitcast.9) | data formatting | bytes 8388608 | tf_op jit(solution)/shard_map/transpose | solution.py:287
  111.6 0.0 copy-start.2
  111.6 1.3 copy-done.2
  112.9 0.0 copy-start.4
  112.9 1.3 copy-done.4
  114.2 25.8 %shard_map.83 = bf16[128,128,128]{2,1,0:T(8,128)(2,1)} custom-call(s32[1024]{0:T(1024)S(1)} %reshape.15.rows_ref, s32[1024]{0:T(1024)S(1)} %reshape.16.starts_ref, f32[80]{0:T(128)S(1)} %pad_maximum_fusion.quad_ref, bf16[40,256,128]{2,1,0:T(8,128)(2,1)S(1)} %bitcast.6, bf16[20,256,128]{2,1,0:T(8,128)(2,1)S(1)} %copy-done.2, ...), custom_call_target="tpu_custom_call" | custom-call | tf_op jit(solution)/shard_map/pallas_call | solution.py:294
Async XLA Ops:
  4.0 1.6 %copy-start = (bf16[64,16,1024]{2,1,0:T(8,128)(2,1)S(1)}, bf16[64,16,1024]{2,1,0:T(8,128)(2,1)}, u32[]{:S(2)}) copy-start(bf16[64,16,1024]{2,1,0:T(8,128)(2,1)} %lat_ref.1) | copy-start | bytes 6291460
  93.7 1.1 copy-start.1
  94.8 1.1 copy-start.3
  111.6 1.3 copy-start.2
  112.9 1.3 copy-start.4

commit v2 on v0

--- a/solution.py
+++ b/solution.py
@@ -11,6 +11,8 @@
 FINE = 64
 MIX_ROWS = 4
 OUT_ROWS = 8
+UNROLL = 4
+MESH = pl.DeviceIdType.MESH
 
 
 def from_behind(block, axis, distance):
@@ -95,9 +97,208 @@
     )(rows, starts, quad, ext, filt, basis_values)
 
 
+def fused(axis, bases, entries, places_ref, quad_ref, lat_ref, filt_ref, values_ref, out_ref, recv, from_left, from_right, pack, go_right, go_left, turned, mixed, sends, recvs, halo_sends, halo_recvs):
+    n = lax.axis_size(axis)
+    me = lax.axis_index(axis)
+    right, left = lax.rem(me + 1, n), lax.rem(me + n - 1, n)
+    pairs = lat_ref.shape[0] // 8
+    sections = lat_ref.shape[0] // (2 * pairs) + 1
+    quads = pairs // 2
+    deep = go_right.shape[1]
+    channels = out_ref.shape[2]
+    row_total = out_ref.shape[0]
+
+    barrier = pltpu.get_barrier_semaphore()
+
+    @pl.loop(1, n)
+    def _(distance):
+        peer = lax.rem(me + distance, n)
+        pl.semaphore_signal(barrier, inc=1, device_id={axis: peer}, device_id_type=MESH)
+
+    pl.semaphore_wait(barrier, n - 1)
+
+    def source(section, target):
+        if section == 1:
+            return pack.at[lax.rem(target + n // 2, n), pl.ds(0, pairs)]
+        return pack.at[target, pl.ds(max(section - 1, 0) * pairs, pairs)]
+
+    def piece(section, target, sender, peer):
+        return pltpu.make_async_remote_copy(
+            src_ref=source(section, target),
+            dst_ref=recv.at[pl.ds(section * pairs, pairs), sender],
+            send_sem=sends.at[section, target],
+            recv_sem=recvs.at[section, sender],
+            device_id={axis: peer},
+            device_id_type=MESH,
+        )
+
+    def halo(section, way):
+        held, landed, peer = (go_right, from_left, right) if way == 0 else (go_left, from_right, left)
+        part = pl.ds(section * quads, quads)
+        return pltpu.make_async_remote_copy(
+            src_ref=held.at[part],
+            dst_ref=landed.at[part],
+            send_sem=halo_sends.at[section, way],
+            recv_sem=halo_recvs.at[section, way],
+            device_id={axis: peer},
+            device_id_type=MESH,
+        )
+
+    for section in range(sections):
+        if section != 1:
+            first = max(section - 1, 0) * pairs
+
+            @pl.loop(first, first + pairs)
+            def _(p):
+                for t in range(n // 2):
+                    a = lat_ref[2 * p, :, t * 128 : (t + 1) * 128]
+                    b = lat_ref[2 * p + 1, :, t * 128 : (t + 1) * 128]
+                    pack[2 * t, p] = jnp.concatenate([a[:, :64], b[:, :64]], axis=1)
+                    pack[2 * t + 1, p] = jnp.concatenate([a[:, 64:], b[:, 64:]], axis=1)
+
+        @pl.loop(1, n)
+        def _(distance):
+            peer = lax.rem(me + distance, n)
+            piece(section, peer, me, peer).start()
+
+        recv[pl.ds(section * pairs, pairs), me] = source(section, me)[...]
+
+    @pl.loop(0, FINE)
+    def _(u):
+        flat = values_ref[:, u].reshape(entries * BLOCK, row_total).astype(jnp.float32).T
+        for part in range(entries * BLOCK // 128):
+            turned[part, pl.ds(u, row_total, stride=FINE), :] = flat[:, part * 128 : (part + 1) * 128]
+
+    def mix(data, first_row, count, to):
+        size = 128 // count
+        product = lax.dot_general(
+            data, filt_ref[...], (((0,), (0,)), ((), ())), preferred_element_type=jnp.float32
+        )
+        for r in range(count):
+            row = first_row + r
+            part = (product[r * size : (r + 1) * size] * quad_ref[row]).astype(jnp.bfloat16)
+            for k in range(bases):
+                for b in range(size // BLOCK):
+                    mixed[(row * bases + k) * 4 + to + b] = part[
+                        b * BLOCK : (b + 1) * BLOCK, k * channels : (k + 1) * channels
+                    ]
+
+    def finish(section):
+        halo(section, 0).wait_recv()
+        halo(section, 1).wait_recv()
+
+        @pl.loop(section * quads, (section + 1) * quads)
+        def _(q):
+            mix(from_left[q], q * 4, 4, 0)
+            mix(from_right[q], q * 4, 4, 3)
+
+    def spread(begin, end):
+        @pl.loop(begin // UNROLL, end // UNROLL)
+        def _(group):
+            for g in range(UNROLL):
+                h = group * UNROLL + g
+                at = [places_ref[h * entries + j] for j in range(entries)]
+                first = jnp.concatenate([mixed[i] for i in at], axis=0)
+                second = jnp.concatenate([mixed[i + 1] for i in at], axis=0)
+                terms = jnp.concatenate([first, second], axis=1)
+                here = pl.ds(pl.multiple_of(h * FINE, FINE), FINE)
+                weights = jnp.concatenate([turned[i, here, :] for i in range(turned.shape[0])], axis=1)
+                total = jnp.dot(weights.astype(jnp.bfloat16), terms, preferred_element_type=jnp.float32)
+                total = total.astype(jnp.bfloat16)
+                out_ref[h, :FINE] = total[:, :channels]
+                out_ref[h, FINE:] = total[:, channels:]
+
+    done = 0
+    for section in range(sections):
+
+        @pl.loop(1, n)
+        def _(distance):
+            peer = lax.rem(me + n - distance, n)
+            piece(section, peer, peer, peer).wait_recv()
+
+        @pl.loop(section * quads, (section + 1) * quads)
+        def _(q):
+            pa = recv[2 * q].reshape(deep, 128)
+            pb = recv[2 * q + 1].reshape(deep, 128)
+            go_right[q] = jnp.concatenate([pa[:, 32:64], pa[:, 96:], pb[:, 32:64], pb[:, 96:]], axis=1)
+            go_left[q] = jnp.concatenate([pa[:, :32], pa[:, 64:96], pb[:, :32], pb[:, 64:96]], axis=1)
+
+        halo(section, 0).start()
+        halo(section, 1).start()
+
+        @pl.loop(section * pairs, (section + 1) * pairs)
+        def _(p):
+            mix(recv[p].reshape(deep, 128), p * 2, 2, 1)
+
+        if section >= 1:
+            finish(section - 1)
+        if section >= 3:
+            ready = 4 * pairs * (section - 1) - 8
+            spread(done, ready)
+            done = ready
+
+    finish(sections - 1)
+    spread(done, row_total)
+    for section in range(sections):
+        halo(section, 0).wait_send()
+        halo(section, 1).wait_send()
+
+        @pl.loop(1, n)
+        def _(distance):
+            peer = lax.rem(me + distance, n)
+            piece(section, peer, me, peer).wait_send()
+
+
+def on_device_packed(
+    latent, filters, quadrature, basis_values, source_row, offset, basis_index, across_pole
+):
+    n = lax.axis_size("lon")
+    source_total = latent.shape[0]
+    row_total, entries = source_row.shape
+    bases, channels, deep = filters.shape
+    pole = source_total // 4
+    place = jnp.where((source_row >= pole) | (across_pole == 1), source_row + pole, source_row)
+    places = ((place * bases + basis_index) * 4 + 1 - offset).reshape(-1)
+    quad = jnp.concatenate([quadrature[:pole], quadrature])
+    filt = filters.reshape(bases * channels, deep).T
+    values = jnp.transpose(basis_values, (1, 2, 3, 0))
+    all_rows = source_total + pole
+    pairs, quads, sections = all_rows // 2, all_rows // 4, 5
+    kind = latent.dtype
+    smem = pl.BlockSpec(memory_space=pltpu.SMEM)
+    vmem = pl.BlockSpec(memory_space=pltpu.VMEM)
+    return pl.pallas_call(
+        functools.partial(fused, "lon", bases, entries),
+        out_shape=jax.ShapeDtypeStruct((row_total, 2 * FINE, channels), kind),
+        in_specs=[smem, smem, vmem, vmem, vmem],
+        out_specs=vmem,
+        scratch_shapes=[
+            pltpu.VMEM((pairs, n, latent.shape[1], 128), kind),
+            pltpu.VMEM((quads, deep, 128), kind),
+            pltpu.VMEM((quads, deep, 128), kind),
+            pltpu.VMEM((n, source_total // 2, latent.shape[1], 128), kind),
+            pltpu.VMEM((quads, deep, 128), kind),
+            pltpu.VMEM((quads, deep, 128), kind),
+            pltpu.VMEM((entries * BLOCK // 128, row_total * FINE, 128), jnp.float32),
+            pltpu.VMEM((all_rows * bases * 4, BLOCK, channels), kind),
+            pltpu.SemaphoreType.DMA((sections, n)),
+            pltpu.SemaphoreType.DMA((sections, n)),
+            pltpu.SemaphoreType.DMA((sections, 2)),
+            pltpu.SemaphoreType.DMA((sections, 2)),
+        ],
+        compiler_params=pltpu.CompilerParams(
+            collective_id=0, has_side_effects=True, vmem_limit_bytes=58 * 2**20
+        ),
+    )(places, quad, latent, filt, values)
+
+
 def solution(mesh):
+    def chosen(latent, *rest):
+        packed = latent.shape[1] % 16 == 0
+        return (on_device_packed if packed else on_device)(latent, *rest)
+
     in_specs = (P("grp", "lon", None), P(), P(), P(), P(), P(), P(), P())
     out_specs = P("grp", "lon", None)
     return jax.shard_map(
-        on_device, mesh=mesh, in_specs=in_specs, out_specs=out_specs, check_vma=False
+        chosen, mesh=mesh, in_specs=in_specs, out_specs=out_specs, check_vma=False
     )

time: 216 us -> 106 us (0.49)
  blocking collectives: 99.7 us -> 0 us
  Pallas kernels: 28.2 us -> 96.3 us
  local copies, waits for them, and re-layouts: 72 us -> 7.69 us
  other arithmetic: 10.2 us -> 2.09 us
  starting transfers between devices: 4.49 us -> 0 us
    all_to_all x1 -> x0, blocking collectives: 99.7 us -> none  [on_device(): lax.all_to_all(stacked, 'lon', split_axis=2, concat_axis=1, tiled=True)]
    pallas_call x1, Pallas kernels: 28.2 us -> 96.3 us  [on_device_packed(): pl.pallas_call(functools.partial(fused, 'lon', bases, entries), out_shape...]
    slice x4 -> x0, local copies, waits for them, and re-layouts: 21.2 us -> none  [the longest x2 14.5 us: on_device(): left = from_behind(tile[:, :, BLOCK:], 'lon', 1)]
    unnamed x11 -> x1, local copies, waits for them, and re-layouts: 23.1 us -> 4.79 us
    all_to_all x1 -> x0, local copies, waits for them, and re-layouts: 11.6 us -> none  [on_device(): lax.all_to_all(stacked, 'lon', split_axis=2, concat_axis=1, tiled=True)]
    ppermute x2 -> x0, local copies, waits for them, and re-layouts: 9.3 us -> none  [from_behind(): return lax.ppermute(block, axis, route)]
    concatenate x3 -> x1, other arithmetic: 10.2 us -> 1.34 us  [on_device_packed(): quad = jnp.concatenate([quadrature[:pole], quadrature])]
    concatenate x1 -> x0, local copies, waits for them, and re-layouts: 5.09 us -> none  [on_device(): stacked = jnp.concatenate([latent, turned], axis=0)]
  transfers between devices with their start and end apart: 2 -> 0, of which waited for: 0 -> 0; matrix products, arithmetic and copies ran while one was open for 16% -> 0% of each run, Pallas kernels for 0% -> 0%
where the time goes in v2:
time: 106 us
  Pallas kernels  96.3 us (91%)
  local copies, waits for them, and re-layouts  7.69 us (7%)
  other arithmetic  2.09 us (2%)
    pallas_call x1, Pallas kernels, on_device_packed(): pl.pallas_call(functools.partial(fused, 'lon', bases, entries), out_shape...  96.3 us
    unnamed x1, local copies, waits for them, and re-layouts  4.79 us

profile of v2, /device:TPU:0, one launch (start us, length us, event | category | flops | bytes accessed | tf_op | source)
XLA Modules:
  0.0 106.1 jit_solution(15347339565810946754)
XLA Ops:
  0.0 1.3 %pad_maximum_fusion.quad_ref = f32[80]{0:T(128)} fusion(f32[64]{0:T(128)} %param.10, f32[16]{0:T(128)} %bitcast.7), kind=kLoop, calls=%fused_computation.6 | loop fusion | flops 80 | bytes 640 | tf_op jit(solution)/shard_map/concatenate | solution.py:262
  1.3 0.7 fusion.4
  2.1 0.1 copy.10
  2.2 0.7 reshape.6.places_ref
  2.9 2.1 %copy.11 = bf16[1152,256]{0,1:T(8,128)(2,1)} copy(bf16[1152,256]{1,0:T(8,128)(2,1)} %bitcast.6) | data formatting | bytes 1179648 | tf_op jit(solution)/shard_map/reshape | solution.py:263
  5.0 96.3 %shard_map.82 = bf16[128,128,128]{2,1,0:T(8,128)(2,1)} custom-call(s32[1024]{0:T(1024)} %reshape.6.places_ref, f32[80]{0:T(128)} %pad_maximum_fusion.quad_ref, bf16[64,16,1024]{2,1,0:T(8,128)(2,1)} %lat_ref.1, bf16[256,1152]{1,0:T(8,128)(2,1)} %bitcast.5, bf16[8,64,32,128]{3,2,1,0:T(8,128)(2,1)} %bitcast.4), custom_call_target="tpu_custom_call" | custom-call | tf_op jit(solution)/shard_map/pallas_call | solution.py:270
  101.3 4.8 %copy.13 = bf16[128,128,128]{2,1,0:T(8,128)(2,1)} copy(bf16[128,128,128]{2,1,0:T(8,128)(2,1)} %shard_map.82) | data formatting | bytes 8388608

commit v3 on v2

--- a/solution.py
+++ b/solution.py
@@ -12,6 +12,7 @@
 MIX_ROWS = 4
 OUT_ROWS = 8
 UNROLL = 4
+AHEAD = 3
 MESH = pl.DeviceIdType.MESH
 
 
@@ -97,7 +98,7 @@
     )(rows, starts, quad, ext, filt, basis_values)
 
 
-def fused(axis, bases, entries, places_ref, quad_ref, lat_ref, filt_ref, values_ref, out_ref, recv, from_left, from_right, pack, go_right, go_left, turned, mixed, sends, recvs, halo_sends, halo_recvs):
+def fused(axis, bases, entries, places_ref, quad_ref, lat_ref, filt_ref, values_hbm, out_ref, values_ref, filt_t, fetch_sem, recv, from_left, from_right, pack, go_right, go_left, turned, mixed, sends, recvs, halo_sends, halo_recvs):
     n = lax.axis_size(axis)
     me = lax.axis_index(axis)
     right, left = lax.rem(me + 1, n), lax.rem(me + n - 1, n)
@@ -108,6 +109,8 @@
     channels = out_ref.shape[2]
     row_total = out_ref.shape[0]
 
+    fetch = pltpu.make_async_copy(values_hbm, values_ref, fetch_sem)
+    fetch.start()
     barrier = pltpu.get_barrier_semaphore()
 
     @pl.loop(1, n)
@@ -144,6 +147,14 @@
             device_id_type=MESH,
         )
 
+    def send(section):
+        @pl.loop(1, n)
+        def _(distance):
+            peer = lax.rem(me + distance * (n // 2 - 1), n)
+            piece(section, peer, me, peer).start()
+
+        recv[pl.ds(section * pairs, pairs), me] = source(section, me)[...]
+
     for section in range(sections):
         if section != 1:
             first = max(section - 1, 0) * pairs
@@ -156,12 +167,12 @@
                     pack[2 * t, p] = jnp.concatenate([a[:, :64], b[:, :64]], axis=1)
                     pack[2 * t + 1, p] = jnp.concatenate([a[:, 64:], b[:, 64:]], axis=1)
 
-        @pl.loop(1, n)
-        def _(distance):
-            peer = lax.rem(me + distance, n)
-            piece(section, peer, me, peer).start()
-
-        recv[pl.ds(section * pairs, pairs), me] = source(section, me)[...]
+        if section < AHEAD:
+            send(section)
+
+    fetch.wait()
+    for k in range(bases):
+        filt_t[:, k * channels : (k + 1) * channels] = filt_ref[k].astype(jnp.float32).T.astype(jnp.bfloat16)
 
     @pl.loop(0, FINE)
     def _(u):
@@ -172,11 +183,12 @@
     def mix(data, first_row, count, to):
         size = 128 // count
         product = lax.dot_general(
-            data, filt_ref[...], (((0,), (0,)), ((), ())), preferred_element_type=jnp.float32
+            data, filt_t[...], (((0,), (0,)), ((), ())), preferred_element_type=jnp.float32
         )
         for r in range(count):
             row = first_row + r
-            part = (product[r * size : (r + 1) * size] * quad_ref[row]).astype(jnp.bfloat16)
+            at = row - jnp.where(row >= 2 * pairs, 2 * pairs, 0)
+            part = (product[r * size : (r + 1) * size] * quad_ref[at]).astype(jnp.bfloat16)
             for k in range(bases):
                 for b in range(size // BLOCK):
                     mixed[(row * bases + k) * 4 + to + b] = part[
@@ -225,6 +237,8 @@
 
         halo(section, 0).start()
         halo(section, 1).start()
+        if section + AHEAD < sections:
+            send(section + AHEAD)
 
         @pl.loop(section * pairs, (section + 1) * pairs)
         def _(p):
@@ -259,8 +273,6 @@
     pole = source_total // 4
     place = jnp.where((source_row >= pole) | (across_pole == 1), source_row + pole, source_row)
     places = ((place * bases + basis_index) * 4 + 1 - offset).reshape(-1)
-    quad = jnp.concatenate([quadrature[:pole], quadrature])
-    filt = filters.reshape(bases * channels, deep).T
     values = jnp.transpose(basis_values, (1, 2, 3, 0))
     all_rows = source_total + pole
     pairs, quads, sections = all_rows // 2, all_rows // 4, 5
@@ -270,9 +282,12 @@
     return pl.pallas_call(
         functools.partial(fused, "lon", bases, entries),
         out_shape=jax.ShapeDtypeStruct((row_total, 2 * FINE, channels), kind),
-        in_specs=[smem, smem, vmem, vmem, vmem],
+        in_specs=[smem, smem, vmem, vmem, pl.BlockSpec(memory_space=pl.ANY)],
         out_specs=vmem,
         scratch_shapes=[
+            pltpu.VMEM(values.shape, kind),
+            pltpu.VMEM((deep, bases * channels), kind),
+            pltpu.SemaphoreType.DMA,
             pltpu.VMEM((pairs, n, latent.shape[1], 128), kind),
             pltpu.VMEM((quads, deep, 128), kind),
             pltpu.VMEM((quads, deep, 128), kind),
@@ -289,7 +304,7 @@
         compiler_params=pltpu.CompilerParams(
             collective_id=0, has_side_effects=True, vmem_limit_bytes=58 * 2**20
         ),
-    )(places, quad, latent, filt, values)
+    )(places, quadrature, latent, filters, values)
 
 
 def solution(mesh):

time: 106 us -> 102 us (0.962)
  local copies, waits for them, and re-layouts: 7.69 us -> 5.57 us
  other arithmetic: 2.09 us -> 0.74 us
    reshape x1 -> x0, local copies, waits for them, and re-layouts: 2.12 us -> none  [on_device_packed(): filt = filters.reshape(bases * channels, deep).T]
    concatenate x1 -> x0, other arithmetic: 1.34 us -> none  [on_device_packed(): quad = jnp.concatenate([quadrature[:pole], quadrature])]
where the time goes in v3:
time: 102 us
  Pallas kernels  95.4 us (94%)
  local copies, waits for them, and re-layouts  5.57 us (5%)
    pallas_call x1, Pallas kernels, on_device_packed(): pl.pallas_call(functools.partial(fused, 'lon', bases, entries), out_shape...  95.4 us
    unnamed x1, local copies, waits for them, and re-layouts  4.79 us

profile of v3, /device:TPU:0, one launch (start us, length us, event | category | flops | bytes accessed | tf_op | source)
XLA Modules:
  0.0 101.7 jit_solution(4245290441039212191)
XLA Ops:
  0.0 0.7 fusion.4
  0.7 0.1 copy.9
  0.8 0.7 reshape.3.places_ref
  1.5 95.4 %shard_map.82 = bf16[128,128,128]{2,1,0:T(8,128)(2,1)} custom-call(s32[1024]{0:T(1024)} %reshape.3.places_ref, f32[64]{0:T(128)} %quad_ref.1, bf16[64,16,1024]{2,1,0:T(8,128)(2,1)} %lat_ref.1, bf16[9,128,256]{2,1,0:T(8,128)(2,1)} %filt_ref.1, bf16[8,64,32,128]{3,2,1,0:T(8,128)(2,1)} %bitcast.1), custom_call_target="tpu_custom_call" | custom-call | tf_op jit(solution)/shard_map/pallas_call | solution.py:282
  96.9 4.8 %copy.11 = bf16[128,128,128]{2,1,0:T(8,128)(2,1)} copy(bf16[128,128,128]{2,1,0:T(8,128)(2,1)} %shard_map.82) | data formatting | bytes 8388608

commit v4 on v3

--- a/solution.py
+++ b/solution.py
@@ -103,8 +103,10 @@
     me = lax.axis_index(axis)
     right, left = lax.rem(me + 1, n), lax.rem(me + n - 1, n)
     pairs = lat_ref.shape[0] // 8
-    sections = lat_ref.shape[0] // (2 * pairs) + 1
-    quads = pairs // 2
+    small = pairs // 2
+    cuts = [(0, pairs, 0), (pairs, pairs, 0), (2 * pairs, pairs, pairs), (3 * pairs, pairs, 2 * pairs)]
+    cuts += [(4 * pairs, small, 3 * pairs), (4 * pairs + small, small, 3 * pairs + small)]
+    sections = len(cuts)
     deep = go_right.shape[1]
     channels = out_ref.shape[2]
     row_total = out_ref.shape[0]
@@ -122,13 +124,13 @@
 
     def source(section, target):
         if section == 1:
-            return pack.at[lax.rem(target + n // 2, n), pl.ds(0, pairs)]
-        return pack.at[target, pl.ds(max(section - 1, 0) * pairs, pairs)]
+            target = lax.rem(target + n // 2, n)
+        return pack.at[target, pl.ds(cuts[section][2], cuts[section][1])]
 
     def piece(section, target, sender, peer):
         return pltpu.make_async_remote_copy(
             src_ref=source(section, target),
-            dst_ref=recv.at[pl.ds(section * pairs, pairs), sender],
+            dst_ref=recv.at[pl.ds(cuts[section][0], cuts[section][1]), sender],
             send_sem=sends.at[section, target],
             recv_sem=recvs.at[section, sender],
             device_id={axis: peer},
@@ -137,7 +139,7 @@
 
     def halo(section, way):
         held, landed, peer = (go_right, from_left, right) if way == 0 else (go_left, from_right, left)
-        part = pl.ds(section * quads, quads)
+        part = pl.ds(cuts[section][0] // 2, cuts[section][1] // 2)
         return pltpu.make_async_remote_copy(
             src_ref=held.at[part],
             dst_ref=landed.at[part],
@@ -153,13 +155,12 @@
             peer = lax.rem(me + distance * (n // 2 - 1), n)
             piece(section, peer, me, peer).start()
 
-        recv[pl.ds(section * pairs, pairs), me] = source(section, me)[...]
+        recv[pl.ds(cuts[section][0], cuts[section][1]), me] = source(section, me)[...]
 
     for section in range(sections):
         if section != 1:
-            first = max(section - 1, 0) * pairs
-
-            @pl.loop(first, first + pairs)
+
+            @pl.loop(cuts[section][2], cuts[section][2] + cuts[section][1])
             def _(p):
                 for t in range(n // 2):
                     a = lat_ref[2 * p, :, t * 128 : (t + 1) * 128]
@@ -199,7 +200,7 @@
         halo(section, 0).wait_recv()
         halo(section, 1).wait_recv()
 
-        @pl.loop(section * quads, (section + 1) * quads)
+        @pl.loop(cuts[section][0] // 2, (cuts[section][0] + cuts[section][1]) // 2)
         def _(q):
             mix(from_left[q], q * 4, 4, 0)
             mix(from_right[q], q * 4, 4, 3)
@@ -228,7 +229,7 @@
             peer = lax.rem(me + n - distance, n)
             piece(section, peer, peer, peer).wait_recv()
 
-        @pl.loop(section * quads, (section + 1) * quads)
+        @pl.loop(cuts[section][0] // 2, (cuts[section][0] + cuts[section][1]) // 2)
         def _(q):
             pa = recv[2 * q].reshape(deep, 128)
             pb = recv[2 * q + 1].reshape(deep, 128)
@@ -240,14 +241,14 @@
         if section + AHEAD < sections:
             send(section + AHEAD)
 
-        @pl.loop(section * pairs, (section + 1) * pairs)
+        @pl.loop(cuts[section][0], cuts[section][0] + cuts[section][1])
         def _(p):
             mix(recv[p].reshape(deep, 128), p * 2, 2, 1)
 
         if section >= 1:
             finish(section - 1)
         if section >= 3:
-            ready = 4 * pairs * (section - 1) - 8
+            ready = 4 * cuts[section][2] - 8
             spread(done, ready)
             done = ready
 
@@ -275,7 +276,7 @@
     places = ((place * bases + basis_index) * 4 + 1 - offset).reshape(-1)
     values = jnp.transpose(basis_values, (1, 2, 3, 0))
     all_rows = source_total + pole
-    pairs, quads, sections = all_rows // 2, all_rows // 4, 5
+    pairs, quads, sections = all_rows // 2, all_rows // 4, 6
     kind = latent.dtype
     smem = pl.BlockSpec(memory_space=pltpu.SMEM)
     vmem = pl.BlockSpec(memory_space=pltpu.VMEM)

time: 102 us -> 103 us (level)
  no operation moved by 1% of the time
where the time goes in v4:
time: 103 us
  Pallas kernels  96.3 us (93%)
  local copies, waits for them, and re-layouts  5.57 us (5%)
    pallas_call x1, Pallas kernels, on_device_packed(): pl.pallas_call(functools.partial(fused, 'lon', bases, entries), out_shape...  96.3 us
    unnamed x1, local copies, waits for them, and re-layouts  4.79 us

profile of v4, /device:TPU:0, one launch (start us, length us, event | category | flops | bytes accessed | tf_op | source)
XLA Modules:
  0.0 102.6 jit_solution(5350003278791760399)
XLA Ops:
  0.0 0.7 fusion.4
  0.7 0.1 copy.9
  0.8 0.7 reshape.3.places_ref
  1.5 96.3 %shard_map.82 = bf16[128,128,128]{2,1,0:T(8,128)(2,1)} custom-call(s32[1024]{0:T(1024)} %reshape.3.places_ref, f32[64]{0:T(128)} %quad_ref.1, bf16[64,16,1024]{2,1,0:T(8,128)(2,1)} %lat_ref.1, bf16[9,128,256]{2,1,0:T(8,128)(2,1)} %filt_ref.1, bf16[8,64,32,128]{3,2,1,0:T(8,128)(2,1)} %bitcast.1), custom_call_target="tpu_custom_call" | custom-call | tf_op jit(solution)/shard_map/pallas_call | solution.py:283
  97.8 4.8 %copy.11 = bf16[128,128,128]{2,1,0:T(8,128)(2,1)} copy(bf16[128,128,128]{2,1,0:T(8,128)(2,1)} %shard_map.82) | data formatting | bytes 8388608

commit v5 on v3

--- a/solution.py
+++ b/solution.py
@@ -12,7 +12,7 @@
 MIX_ROWS = 4
 OUT_ROWS = 8
 UNROLL = 4
-AHEAD = 3
+AHEAD = 2
 MESH = pl.DeviceIdType.MESH
 
 

time: 102 us -> 102 us (level)
  no operation moved by 1% of the time
where the time goes in v5:
time: 102 us; the launch traced here: 101 us
  Pallas kernels  94.5 us (93%)
  local copies, waits for them, and re-layouts  5.57 us (5%)
    pallas_call x1, Pallas kernels, on_device_packed(): pl.pallas_call(functools.partial(fused, 'lon', bases, entries), out_shape...  94.5 us
    unnamed x1, local copies, waits for them, and re-layouts  4.79 us

profile of v5, /device:TPU:0, one launch (start us, length us, event | category | flops | bytes accessed | tf_op | source)
XLA Modules:
  0.0 100.8 jit_solution(413759600920869148)
XLA Ops:
  0.0 0.7 fusion.4
  0.7 0.1 copy.9
  0.8 0.7 reshape.3.places_ref
  1.5 94.5 %shard_map.82 = bf16[128,128,128]{2,1,0:T(8,128)(2,1)} custom-call(s32[1024]{0:T(1024)} %reshape.3.places_ref, f32[64]{0:T(128)} %quad_ref.1, bf16[64,16,1024]{2,1,0:T(8,128)(2,1)} %lat_ref.1, bf16[9,128,256]{2,1,0:T(8,128)(2,1)} %filt_ref.1, bf16[8,64,32,128]{3,2,1,0:T(8,128)(2,1)} %bitcast.1), custom_call_target="tpu_custom_call" | custom-call | tf_op jit(solution)/shard_map/pallas_call | solution.py:282
  96.0 4.8 %copy.11 = bf16[128,128,128]{2,1,0:T(8,128)(2,1)} copy(bf16[128,128,128]{2,1,0:T(8,128)(2,1)} %shard_map.82) | data formatting | bytes 8388608
